TPU v7x, 32 devices: a whole 2x2x4 slice. The times are simulated.
32 devices in a mesh: pole: 2 (over y), prow: 8 (over z, x), pcol: 2 (over core).
Axes of the slice: x: 2, y: 2, z: 4, core: 2. Of those that a mesh axis runs over, the one named last changes fastest.
Arguments:
- ancestor_inverse: float32 [2048, 1024], P(('pole', 'prow'), 'pcol'), parts along dimension 0, as said below
- pivots_one: float32 [8, 128, 128], P(('pole', 'pcol')), parts along dimension 0, may hold values from -6 to 6
- factor_one: float32 [2048, 512], P(('pole', 'prow'), 'pcol'), parts along dimension 0, may hold values from -0.25 to 0.25
- pattern_one: int32 [16, 4], P(('pole', 'prow')), parts along dimension 0, may hold values 0 or 1
- pivots_zero: float32 [16, 128, 128], P(('pole', 'pcol')), parts along dimension 0, may hold values from -6 to 6
- factor_zero: float32 [2048, 1024], P(('pole', 'prow'), 'pcol'), parts along dimension 0, may hold values from -0.375 to 0.375
- factor_parent: float32 [16, 128, 128], P(('pole', 'pcol')), parts along dimension 0, may hold values from -0.5 to 0.5
- parent_index: int32 [16], P(('pole', 'pcol')), parts along dimension 0, may hold values from 0 to 3
- pattern_zero: int32 [16, 8], P(('pole', 'prow'), 'pcol'), parts along dimension 0, may hold values 0 or 1
Outputs:
- cross_one: float32 [2048, 512], P(('pole', 'prow'), 'pcol'), parts along dimension 0
- diag_one: float32 [8, 128, 128], P(('pole', 'pcol')), parts along dimension 0
- cross_zero: float32 [2048, 1024], P(('pole', 'prow'), 'pcol'), parts along dimension 0
- parent_zero: float32 [16, 128, 128], P(('pole', 'pcol')), parts along dimension 0
- diag_zero: float32 [16, 128, 128], P(('pole', 'pcol')), parts along dimension 0
There are 2 independent parts, one for each index of `pole`. A program takes and returns all parts, laid end to end along the dimension named above; each array names one. Nothing has to cross between parts.
Inputs may be any that keep to these rules, and one draw needn't show every extreme that they name: ancestor_inverse is symmetric up to rounding.
All inputs are finite; a program needn't handle non-finite values. No bound on the sum of `pattern_one` or of `pattern_zero` on one device may be relied on, other than what follows from the above.
Results may differ from a plain program's by a relative error of at most 0.000073.
Values sent between devices are 32-bit elements; how exact they have to be, the bound alone decides.
A program may use at most 128 MiB of HBM per device.

v0:
```python
import jax
import jax.numpy as jnp
from jax import lax
from jax.sharding import PartitionSpec as P


def expand_mask(pattern, width):
    return jnp.repeat(jnp.repeat(pattern, width, 0), width, 1)


def local(
    ancestor_inverse,
    pivots_one,
    factor_one,
    pattern_one,
    pivots_zero,
    factor_zero,
    factor_parent,
    parent_index,
    pattern_zero,
):
    highest = lax.Precision.HIGHEST
    band = lax.all_gather(ancestor_inverse, "pcol", axis=1, tiled=True)
    width = pivots_one.shape[1]
    rows = band.shape[0]
    one_local = pivots_one.shape[0]
    zero_local = pivots_zero.shape[0]
    column = lax.axis_index("pcol")
    total_one = one_local * lax.axis_size("pcol")
    pattern_float = pattern_one.astype(jnp.float32)
    own_pattern = lax.dynamic_slice_in_dim(pattern_float, column * one_local, one_local, 1)
    level_one = factor_one * expand_mask(own_pattern, width)
    selector = (parent_index[:, None] == jnp.arange(total_one, dtype=jnp.int32)[None, :]).astype(
        jnp.float32
    )
    parent_pattern = jnp.dot(
        pattern_float, selector.T, precision=highest, preferred_element_type=jnp.float32
    )
    child_pattern = pattern_zero.astype(jnp.float32) * parent_pattern
    child_mask = expand_mask(child_pattern, width)
    level_zero = factor_zero * child_mask

    def add_rows(piece):
        return jnp.dot(band, piece, precision=highest, preferred_element_type=jnp.float32)

    product_one = add_rows(lax.all_gather(level_one, "prow", axis=0, tiled=True))
    product_zero = add_rows(lax.all_gather(level_zero, "prow", axis=0, tiled=True))
    cross_full = -product_one
    shaped_one = level_one.reshape(rows, one_local, width)
    diag_partial = jnp.einsum(
        "akb,akc->kbc",
        shaped_one,
        cross_full.reshape(rows, one_local, width),
        precision=highest,
        preferred_element_type=jnp.float32,
    )
    diag_sum = lax.psum(diag_partial, "prow")
    diag_one = pivots_one - diag_sum
    cross_all, diag_all = (
        lax.all_gather(cross_full, "pcol", axis=1, tiled=True),
        lax.all_gather(diag_one, "pcol", axis=0, tiled=True),
    )
    parent_cols = jnp.einsum(
        "anb,cn->acb",
        cross_all.reshape(rows, total_one, width),
        selector,
        precision=highest,
        preferred_element_type=jnp.float32,
    )
    cross_child = -product_zero.reshape(rows, zero_local, width) - jnp.einsum(
        "acb,cbd->acd",
        parent_cols,
        factor_parent,
        precision=highest,
        preferred_element_type=jnp.float32,
    )
    shaped_zero = level_zero.reshape(rows, zero_local, width)
    parent_partial = jnp.einsum(
        "acb,acd->cbd",
        parent_cols,
        shaped_zero,
        precision=highest,
        preferred_element_type=jnp.float32,
    )
    child_partial = jnp.einsum(
        "acb,acd->cbd",
        shaped_zero,
        cross_child,
        precision=highest,
        preferred_element_type=jnp.float32,
    )
    parent_sum, child_sum = lax.psum((parent_partial, child_partial), "prow")
    parents_inv = jnp.einsum(
        "cn,nbd->cbd", selector, diag_all, precision=highest, preferred_element_type=jnp.float32
    )
    parent_zero = -parent_sum - jnp.einsum(
        "cbe,ced->cbd",
        parents_inv,
        factor_parent,
        precision=highest,
        preferred_element_type=jnp.float32,
    )
    diag_zero = (
        pivots_zero
        - child_sum
        - jnp.einsum(
            "cba,cbd->cad",
            factor_parent,
            parent_zero,
            precision=highest,
            preferred_element_type=jnp.float32,
        )
    )
    cross_one = cross_full * expand_mask(own_pattern, width)
    cross_zero = cross_child.reshape(rows, zero_local * width) * child_mask
    return (cross_one, diag_one, cross_zero, parent_zero, diag_zero)


def solution(mesh):
    in_specs = (
        P(("pole", "prow"), "pcol"),
        P(("pole", "pcol"), None, None),
        P(("pole", "prow"), "pcol"),
        P(("pole", "prow"), None),
        P(("pole", "pcol"), None, None),
        P(("pole", "prow"), "pcol"),
        P(("pole", "pcol"), None, None),
        P(("pole", "pcol")),
        P(("pole", "prow"), "pcol"),
    )
    out_specs = (
        P(("pole", "prow"), "pcol"),
        P(("pole", "pcol"), None, None),
        P(("pole", "prow"), "pcol"),
        P(("pole", "pcol"), None, None),
        P(("pole", "pcol"), None, None),
    )
    return jax.shard_map(local, mesh=mesh, in_specs=in_specs, out_specs=out_specs, check_vma=False)
```

profile of v0, /device:TPU:0, one launch (start us, length us, event | category | flops | bytes accessed | tf_op | source)
XLA Modules:
  0.0 196.3 jit_solution(2236936271133507361)
XLA Ops:
  7.2 0.0 copy-start
  7.2 0.0 copy-start.4
  7.2 0.0 all-gather.3.cloned.1.call-start
  7.2 0.7 convert_element_type.7
  8.0 0.1 dynamic-slice_bitcast_fusion
  8.0 0.1 broadcast_bitcast_fusion.1
  8.1 1.0 copy.27
  9.1 0.8 broadcast_multiply_fusion.3
  9.9 0.0 all-gather.3.cloned.1.call-update
  9.9 0.0 all-gather.5.cloned.1.call-start
  9.9 0.9 fusion.2
  10.8 0.1 broadcast_bitcast_fusion
  10.9 1.7 broadcast_multiply_fusion.1
  12.6 0.0 all-gather.5.cloned.1.call-update
  12.6 0.0 copy-start.8
  12.6 0.0 all-reduce.3.cloned.1.call-start
  12.7 1.1 copy.47
  13.7 0.0 copy-done.4
  13.7 2.3 %all_gather.16 = f32[128,1024]{1,0:T(8,128)S(1)} all-gather(f32[128,512]{1,0:T(8,128)S(1)} %copy-done.4), channel_id=1, replica_groups=mesh['pole'=2,'prow'=8,'pcol'=2] {'pcol'}, dimensions={1}, use_global_device_ids=true | all-gather | bytes 786432 | tf_op jit(solution)/shard_map/all_gather | solution.py:23
  16.0 0.0 copy-start.1
  16.0 36.9 %all-gather.3.cloned.1.call-done = f32[1024,256]{0,1:T(8,128)} async-done(((f32[128,256]{0,1:T(8,128)}), f32[1024,256]{0,1:T(8,128)}) %all-gather.3.cloned.1.call-update) | async-done | bytes 1048592 | tf_op jit(solution)/shard_map/all_gather | solution.py:46
  52.9 2.2 %broadcast_multiply_fusion.2 = (f32[128,256]{0,1:T(8,128)S(1)}, f32[256,128]{1,0:T(8,128)S(1)}) fusion(f32[256]{0:T(256)S(1)} %broadcast_bitcast_fusion.1, f32[1024,256]{0,1:T(8,128)} %all-gather.3.cloned.1.call-done, f32[128,1024]{1,0:T(8,128)S(1)} %all_gather.16), kind=kOutput, calls=%fused_computation.15 | convolution fusion | flops 402718720 | bytes 1836032 | tf_op jit(solution)/shard_map/dot_general | solution.py:44
  55.1 2.0 %all_gather.18 = f32[128,512]{0,1:T(8,128)S(1)} all-gather(f32[128,256]{0,1:T(8,128)S(1)} %bitcast.57), channel_id=1, replica_groups=mesh['pole'=2,'prow'=8,'pcol'=2] {'pcol'}, dimensions={1}, use_global_device_ids=true | all-gather | bytes 393216 | tf_op jit(solution)/shard_map/all_gather | solution.py:60
  57.1 0.1 copy.29
  57.3 0.0 copy-done.8
  57.3 0.4 convolution_bitcast_fusion.2
  57.7 0.1 copy.33
  57.9 0.0 copy-done.1
  57.9 1.0 fusion.14
  58.9 1.4 fusion.15
  60.3 43.6 %all-gather.5.cloned.1.call-done = f32[1024,512]{1,0:T(8,128)} async-done(((f32[128,512]{1,0:T(8,128)}), f32[1024,512]{1,0:T(8,128)}) %all-gather.5.cloned.1.call-update) | async-done | bytes 2097168 | tf_op jit(solution)/shard_map/all_gather | solution.py:47
  103.8 5.0 %convolution_negate_fusion = f32[512,128]{1,0:T(8,128)S(1)} fusion(f32[1024,512]{1,0:T(8,128)} %all-gather.5.cloned.1.call-done, f32[128,1024]{1,0:T(8,128)S(1)} %all_gather.16), kind=kOutput, calls=%fused_computation.6 | convolution fusion | flops 805371904 | bytes 2883584 | tf_op jit(solution)/shard_map/dot_general | solution.py:44
  108.8 0.0 copy-start.7
  108.8 0.0 copy-done
  108.9 0.6 fusion.1
  109.5 1.4 fusion.16
  110.8 0.0 copy-start.5
  110.8 0.0 all-reduce.3.cloned.1.call-update
  110.8 0.8 copy.39
  111.6 0.1 copy.32
  111.7 0.7 broadcast_multiply_fusion
  112.5 71.1 %all-reduce.3.cloned.1.call-done = (f32[2,128,128]{2,1,0:T(8,128)}, f32[4,128,128]{2,1,0:T(8,128)}, f32[4,128,128]{2,1,0:T(8,128)}) async-done(((f32[2,128,128]{2,1,0:T(8,128)}, f32[4,128,128]{2,1,0:T(8,128)}, f32[4,128,128]{2,1,0:T(8,128)}), (f32[2,128,128]{2,1,0:T(8,128)}, f32[4,128,128]{2,1,0:T(8,128)}, f32[4,128,128]{2,1,0:T(8,128)})) %all-reduce.3.cloned.1.call-update) | async-done | bytes 655376 | tf_op jit(solution)/shard_map/psum | solution.py:57
  183.5 0.0 copy-start.6
  183.5 0.0 copy-done.7
  183.5 1.0 sub.15
  184.5 0.0 copy-start.3
  184.5 2.0 %all_gather.19 = f32[4,128,128]{2,1,0:T(8,128)S(1)} all-gather(f32[2,128,128]{2,1,0:T(8,128)S(1)} %sub.15), channel_id=1, replica_groups=mesh['pole'=2,'prow'=8,'pcol'=2] {'pcol'}, dimensions={0}, use_global_device_ids=true | all-gather | bytes 393216 | tf_op jit(solution)/shard_map/all_gather | solution.py:61
  186.5 0.5 fusion.4
  187.0 1.4 convolution_subtract_fusion
  188.4 0.0 copy-start.2
  188.4 0.0 copy-done.5
  188.4 0.0 copy-done.6
  188.4 1.3 fusion
  189.7 0.0 copy-done.3
  189.7 0.0 copy-done.2
Async XLA Ops:
  7.2 101.7 %copy-start = (f32[4,128,128]{2,1,0:T(8,128)S(1)}, f32[4,128,128]{2,1,0:T(8,128)}, u32[]{:S(2)}) copy-start(f32[4,128,128]{2,1,0:T(8,128)} %param.15) | copy-start | bytes 786436
  7.2 6.6 %copy-start.4 = (f32[128,512]{1,0:T(8,128)S(1)}, f32[128,512]{1,0:T(8,128)}, u32[]{:S(2)}) copy-start(f32[128,512]{1,0:T(8,128)} %param.9) | copy-start | bytes 786436
  7.2 45.7 %all-gather.3.cloned.1.call-start = ((), (), s32[]{:S(2)}) async-start(), calls=%async_computation | async-start | bytes 1179648 | tf_op jit(solution)/shard_map/all_gather | solution.py:46
  9.9 93.9 %all-gather.5.cloned.1.call-start = ((), (), s32[]{:S(2)}) async-start(), calls=%async_computation.1 | async-start | bytes 2359296 | tf_op jit(solution)/shard_map/all_gather | solution.py:47
  12.6 44.7 %copy-start.8 = (s32[4]{0:T(128)S(1)}, s32[4]{0:T(128)}, u32[]{:S(2)}) copy-start(s32[4]{0:T(128)} %param.16) | copy-start | bytes 52
  12.6 170.9 %all-reduce.3.cloned.1.call-start = ((), (), s32[]{:S(2)}) async-start(), calls=%async_computation.2 | async-start | bytes 1310720 | tf_op jit(solution)/shard_map/psum | solution.py:57
  16.0 41.8 %copy-start.1 = (f32[128,256]{0,1:T(8,128)S(1)}, f32[128,256]{0,1:T(8,128)}, u32[]{:S(2)}) copy-start(f32[128,256]{0,1:T(8,128)} %broadcast_multiply_fusion.3) | copy-start | bytes 393220
  108.8 74.7 %copy-start.7 = (f32[2,128,128]{2,1,0:T(8,128)S(1)}, f32[2,128,128]{2,1,0:T(8,128)}, u32[]{:S(2)}) copy-start(f32[2,128,128]{2,1,0:T(8,128)} %param.10) | copy-start | bytes 393220
  110.8 77.6 %copy-start.5 = (f32[4,128,128]{2,1,0:T(8,128)S(1)}, f32[4,128,128]{2,1,0:T(8,128)}, u32[]{:S(2)}) copy-start(f32[4,128,128]{2,1,0:T(8,128)} %param.13) | copy-start | bytes 786436
  183.5 4.9 %copy-start.6 = (f32[4,128,128]{2,1,0:T(8,128)S(1)}, f32[4,128,128]{2,1,0:T(8,128)}, u32[]{:S(2)}) copy-start(f32[4,128,128]{2,1,0:T(8,128)} %get-tuple-element.17) | copy-start | bytes 786436
  184.5 5.2 %copy-start.3 = (f32[2,128,128]{2,1,0:T(8,128)}, f32[2,128,128]{2,1,0:T(8,128)S(1)}, u32[]{:S(2)}) copy-start(f32[2,128,128]{2,1,0:T(8,128)S(1)} %sub.15) | copy-start | bytes 393220
  188.4 1.3 copy-start.2
Sparse Core Ops, SparseCore 0:
  10.6 42.2 all-gather.2
  55.6 48.1 all-gather.4
  111.0 72.5 all-reduce.2
where the time goes:
time: 197 us; the launch traced here: 196 us
  waiting for transfers between devices  152 us (77%)
  matrix products  16 us (8%)
  between operations  13.9 us (7%)
  blocking collectives  6.25 us (3%)
  other arithmetic  4.85 us (2%)
  local copies, waits for them, and re-layouts  3.51 us (2%)
    psum x1, waiting for transfers between devices, local(): diag_sum = lax.psum(diag_partial, 'prow')  71.1 us
    all_gather x1, waiting for transfers between devices, local(): lax.all_gather(level_zero, 'prow', axis=0, tiled=True)  43.6 us
    all_gather x1, waiting for transfers between devices, local(): lax.all_gather(level_one, 'prow', axis=0, tiled=True)  36.9 us
    dot_general x2, matrix products, add_rows(): jnp.dot(band, piece, precision=highest, preferred_element_type=jnp.float32)  7.22 us
  transfers between devices with their start and end apart: 3, of which 3 were waited for; matrix products, arithmetic and copies ran while one was open for 5% of the time, Pallas kernels for 0%

commit v1 on v0

--- a/solution.py
+++ b/solution.py
@@ -1,6 +1,8 @@
 import jax
 import jax.numpy as jnp
 from jax import lax
+from jax.experimental import pallas as pl
+from jax.experimental.pallas import tpu as pltpu
 from jax.sharding import PartitionSpec as P
 
 
@@ -116,6 +118,273 @@
     return (cross_one, diag_one, cross_zero, parent_zero, diag_zero)
 
 
+RING = 8
+OWN = 3
+HALF = 5
+
+
+def split(x):
+    high = x.astype(jnp.bfloat16)
+    return high, (x - high.astype(jnp.float32)).astype(jnp.bfloat16)
+
+
+def dot3(a, b, dims=((1,), (0,))):
+    def one(x, y):
+        return lax.dot_general(x, y, (dims, ((), ())), preferred_element_type=jnp.float32)
+
+    return one(a[0], b[0]) + (one(a[0], b[1]) + one(a[1], b[0]))
+
+
+def natural(place):
+    return 2 * place + (place // 4) * (15 - 4 * place)
+
+
+def kernel(
+    inverse, pivots_one, factor_one, pattern_one, pivots_zero, factor_zero, factor_parent, parent, pattern_zero,
+    cross_one, diag_one, cross_zero, parent_zero, diag_zero,
+    row, ones, ones_other, zeros, band, a_high, a_low, l_high, l_low, one_high, one_low, z, row_one, sums_one,
+    ring_send, ring_recv, pair_send, pair_recv,
+):
+    w = pivots_one.shape[1]
+    half_row = w // 2
+    pole, prow, q = lax.axis_index("pole"), lax.axis_index("prow"), lax.axis_index("pcol")
+    z_at, x_at = prow // 2, prow % 2
+    place = z_at + x_at * (RING - 1 - 2 * z_at)
+    right = (pole, natural((place + 1) % RING), q)
+    left = (pole, natural((place + RING - 1) % RING), q)
+    other = (pole, prow, 1 - q)
+
+    barrier = pltpu.get_barrier_semaphore()
+    for peer in (left, right, other):
+        pl.semaphore_signal(barrier, inc=1, device_id=peer, device_id_type=pl.DeviceIdType.MESH)
+
+    def block(k):
+        return slice(k * w, (k + 1) * w)
+
+    def flag(value):
+        return value.astype(jnp.float32)
+
+    mask_one = [flag(pattern_one[0, 2 * q + k]) for k in range(2)]
+    parents = [parent[c] for c in range(4)]
+    parent_mask = [sum(flag(p == k) * flag(pattern_one[0, k]) for k in range(4)) for p in parents]
+    mask_zero = [flag(pattern_zero[0, c]) * parent_mask[c] for c in range(4)]
+    for k in range(2):
+        ones[OWN, :, block(k)] = factor_one[:, block(k)] * mask_one[k]
+    for c in range(4):
+        zeros[OWN, :, block(c)] = factor_zero[:, block(c)] * mask_zero[c]
+
+    def copy(src, dst, send, recv, peer):
+        return pltpu.make_async_remote_copy(
+            src_ref=src, dst_ref=dst, send_sem=send, recv_sem=recv,
+            device_id=peer, device_id_type=pl.DeviceIdType.MESH,
+        )
+
+    def to_ring(way, step, chunk):
+        sign = -1 if way == 0 else 1
+        source, target = OWN + sign * (step - 1), (OWN + sign * step) % RING
+        ref = (ones, zeros, band)[chunk]
+        src, dst = ref.at[source], ref.at[target]
+        if chunk == 2:
+            src, dst = ref.at[source, q], ref.at[target, q]
+        place_at = (way, step - 1, chunk)
+        return copy(src, dst, ring_send.at[place_at], ring_recv.at[place_at], right if way == 0 else left)
+
+    def to_pair(kind, slot):
+        if kind == 0:
+            src, dst = ones.at[slot], ones_other.at[slot]
+        elif kind == 1:
+            src, dst = band.at[slot, q], band.at[slot, q]
+        elif slot == 0:
+            src, dst = inverse, row.at[q]
+        elif slot == 1:
+            src, dst = row_one.at[pl.ds(2 * q, 2)], row_one.at[pl.ds(2 * q, 2)]
+        else:
+            src, dst = sums_one.at[pl.ds(2 * q, 2)], sums_one.at[pl.ds(2 * q, 2)]
+        return copy(src, dst, pair_send.at[kind, slot], pair_recv.at[kind, slot], other)
+
+    started = []
+
+    def start(made):
+        made.start()
+        started.append(made)
+
+    pl.semaphore_wait(barrier, 3)
+    start(to_pair(2, 0))
+    for chunk in (0, 1):
+        for way in (0, 1):
+            start(to_ring(way, 1, chunk))
+    start(to_pair(0, OWN))
+
+    row[q] = inverse[...]
+    to_pair(2, 0).wait_recv()
+    for d in range(HALF):
+        column = natural((place + d) % RING)
+        source = (column // 4, slice(None), pl.ds(pl.multiple_of((column % 4) * w, w), w))
+        piece = row[source]
+        for h in range(2):
+            band[OWN, h, :, block(d)] = piece[h * half_row : (h + 1) * half_row]
+    for way in (0, 1):
+        start(to_ring(way, 1, 2))
+
+    def take_band(t):
+        for d in range(HALF):
+            piece = jnp.concatenate([band[t, h, :, block(d)] for h in range(2)], axis=0)
+            u = (t + d) % RING
+            a_high[block(t), block(u)], a_low[block(t), block(u)] = split(piece)
+            if 0 < d < HALF - 1:
+                a_high[block(u), block(t)], a_low[block(u), block(t)] = split(piece.T)
+
+    def take_ones(t):
+        high, low = split(ones[t])
+        l_high[block(t), : 2 * w], l_low[block(t), : 2 * w] = high, low
+        for k in range(2):
+            one_high[2 * q + k, block(t), :] = high[:, block(k)]
+            one_low[2 * q + k, block(t), :] = low[:, block(k)]
+
+    def take_other(t):
+        high, low = split(ones_other[t])
+        for k in range(2):
+            one_high[2 * (1 - q) + k, block(t), :] = high[:, block(k)]
+            one_low[2 * (1 - q) + k, block(t), :] = low[:, block(k)]
+
+    def take_zeros(t):
+        l_high[block(t), 2 * w :], l_low[block(t), 2 * w :] = split(zeros[t])
+
+    def times(rows, lo, hi):
+        inner = slice(lo * w, hi * w)
+        return dot3((a_high[rows, inner], a_low[rows, inner]), (l_high[inner, :], l_low[inner, :]))
+
+    def add_old(lo, hi, new):
+        @pl.loop(lo, hi)
+        def _(t):
+            rows = pl.ds(pl.multiple_of(t * w, w), w)
+            total = z[rows, :]
+            for n in new:
+                total = total + times(rows, n, n + 1)
+            z[rows, :] = total
+
+    take_ones(OWN)
+    take_zeros(OWN)
+    take_band(OWN)
+    z[block(OWN), :] = times(block(OWN), OWN, OWN + 1)
+
+    for step in range(1, 4):
+        last = step == 3
+        for chunk in (0, 1, 2):
+            for way in (0, 1):
+                to_ring(way, step, chunk).wait_recv()
+                t = OWN - step if way == 0 else OWN + step
+                if not last or (chunk == 1) == (way == 0):
+                    start(to_ring(way, step + 1, chunk))
+                if chunk == 0:
+                    start(to_pair(0, t))
+                if chunk == 2:
+                    start(to_pair(1, t))
+        new = (OWN - step, OWN + step)
+        if step == 1:
+            to_pair(0, OWN).wait_recv()
+            take_other(OWN)
+        for t in new:
+            take_ones(t)
+            take_zeros(t)
+            to_pair(0, t).wait_recv()
+            take_other(t)
+            to_pair(1, t).wait_recv()
+            take_band(t)
+        for t in new:
+            z[block(t), :] = times(block(t), OWN - step, OWN + step + 1)
+        add_old(OWN - step + 1, OWN + step, new)
+
+    far = RING - 1
+    to_ring(1, 4, 0).wait_recv()
+    start(to_pair(0, far))
+    take_ones(far)
+    to_ring(1, 4, 2).wait_recv()
+    start(to_pair(1, far))
+    to_ring(0, 4, 1).wait_recv()
+    take_zeros(far)
+    to_pair(0, far).wait_recv()
+    take_other(far)
+    to_pair(1, far).wait_recv()
+    take_band(far)
+    add_old(0, far, (far,))
+    z[block(far), :] = times(block(far), 0, RING)
+
+    for k in range(2):
+        row_one[2 * q + k] = z[block(OWN), block(k)]
+    start(to_pair(2, 1))
+    across = ((0,), (0,))
+    for k in range(2):
+        own = (l_high[:, block(k)], l_low[:, block(k)])
+        made = pivots_one[k] + dot3(own, split(z[:, block(k)]), across)
+        diag_one[k] = made
+        sums_one[2 * q + k] = made
+    start(to_pair(2, 2))
+    for k in range(2):
+        cross_one[:, block(k)] = -z[block(OWN), block(k)] * mask_one[k]
+
+    for c in range(4):
+        at = block(2 + c)
+        product = split(z[:, at])
+        p = parents[c]
+        zeros_c = (l_high[:, at], l_low[:, at])
+        parent_zero[c] = dot3((one_high[p], one_low[p]), product, across)
+        diag_zero[c] = pivots_zero[c] + dot3(zeros_c, product, across)
+
+    to_pair(2, 1).wait_recv()
+    to_pair(2, 2).wait_recv()
+    for c in range(4):
+        p = parents[c]
+        factor = split(factor_parent[c])
+        lift = dot3(split(row_one[p]), factor)
+        cross_zero[:, block(c)] = (lift - z[block(OWN), block(2 + c)]) * mask_zero[c]
+        weight = parent_zero[c]
+        sums = weight - dot3(split(sums_one[p]), factor)
+        parent_zero[c] = sums
+        diag_zero[c] = diag_zero[c] - dot3(split(weight), factor, across) - dot3(factor, split(sums), across)
+
+    for made in started:
+        made.wait_send()
+
+
+def fused(*args):
+    inverse, pivots_one, factor_one, _, pivots_zero, factor_zero, factor_parent, _, _ = args
+    w = pivots_one.shape[1]
+    rows = RING * w
+    f32, b16 = jnp.float32, jnp.bfloat16
+    vmem, smem = pl.BlockSpec(memory_space=pltpu.VMEM), pl.BlockSpec(memory_space=pltpu.SMEM)
+    outs = (factor_one, pivots_one, factor_zero, factor_parent, pivots_zero)
+    return pl.pallas_call(
+        kernel,
+        out_shape=tuple(jax.ShapeDtypeStruct(x.shape, f32) for x in outs),
+        in_specs=[vmem, vmem, vmem, smem, vmem, vmem, vmem, smem, smem],
+        out_specs=(vmem,) * 5,
+        scratch_shapes=[
+            pltpu.VMEM((2, w, 4 * w), f32),
+            pltpu.VMEM((RING, w, 2 * w), f32),
+            pltpu.VMEM((RING, w, 2 * w), f32),
+            pltpu.VMEM((RING, w, 4 * w), f32),
+            pltpu.VMEM((RING, 2, w // 2, HALF * w), f32),
+            pltpu.VMEM((rows, rows), b16),
+            pltpu.VMEM((rows, rows), b16),
+            pltpu.VMEM((rows, 6 * w), b16),
+            pltpu.VMEM((rows, 6 * w), b16),
+            pltpu.VMEM((4, rows, w), b16),
+            pltpu.VMEM((4, rows, w), b16),
+            pltpu.VMEM((rows, 6 * w), f32),
+            pltpu.VMEM((4, w, w), f32),
+            pltpu.VMEM((4, w, w), f32),
+            pltpu.SemaphoreType.DMA((2, 4, 3)),
+            pltpu.SemaphoreType.DMA((2, 4, 3)),
+            pltpu.SemaphoreType.DMA((3, RING)),
+            pltpu.SemaphoreType.DMA((3, RING)),
+        ],
+        compiler_params=pltpu.CompilerParams(
+            collective_id=0, has_side_effects=True, vmem_limit_bytes=48 * 1024 * 1024
+        ),
+    )(*args)
+
+
 def solution(mesh):
     in_specs = (
         P(("pole", "prow"), "pcol"),
@@ -135,4 +404,5 @@
         P(("pole", "pcol"), None, None),
         P(("pole", "pcol"), None, None),
     )
-    return jax.shard_map(local, mesh=mesh, in_specs=in_specs, out_specs=out_specs, check_vma=False)
+    ring = (mesh.shape["prow"], mesh.shape["pcol"]) == (RING, 2)
+    return jax.shard_map(fused if ring else local, mesh=mesh, in_specs=in_specs, out_specs=out_specs, check_vma=False)

time: 197 us -> 68.8 us (0.35)
  waiting for transfers between devices: 152 us -> 0 us
  Pallas kernels: 0 us -> 56.9 us
  matrix products: 16 us -> 0 us
  between operations: 13.9 us -> 0.66 us
  local copies, waits for them, and re-layouts: 3.51 us -> 11 us
  blocking collectives: 6.25 us -> 0 us
  other arithmetic: 4.85 us -> 0 us
    all_gather x2 -> x0, waiting for transfers between devices: 80.5 us -> none  [the longest x1 43.6 us: local(): lax.all_gather(level_zero, 'prow', axis=0, tiled=True)]
    psum x1 -> x0, waiting for transfers between devices: 71.1 us -> none  [local(): diag_sum = lax.psum(diag_partial, 'prow')]
    pallas_call x0 -> x1, Pallas kernels: none -> 56.9 us  [fused(): pl.pallas_call(kernel, out_shape=tuple((jax.ShapeDtypeStruct(x.shape, f32...]
    dot_general x11 -> x0, matrix products: 16 us -> none  [the longest x2 7.22 us: add_rows(): jnp.dot(band, piece, precision=highest, preferred_element_type=jnp.float32)]
    unnamed x20 -> x23, local copies, waits for them, and re-layouts: 1.8 us -> 11 us
    all_gather x3 -> x0, blocking collectives: 6.25 us -> none  [the longest x1 2.26 us: local(): band = lax.all_gather(ancestor_inverse, 'pcol', axis=1, tiled=True)]
    mul x3 -> x0, other arithmetic: 3.17 us -> none  [the longest x1 1.68 us: local(): level_zero = factor_zero * child_mask]
  transfers between devices with their start and end apart: 3 -> 0, of which waited for: 3 -> 0; matrix products, arithmetic and copies ran while one was open for 5% -> 0% of each run, Pallas kernels for 0% -> 0%
where the time goes in v1:
time: 68.8 us; the launch traced here: 68.5 us
  Pallas kernels  56.9 us (83%)
  local copies, waits for them, and re-layouts  11 us (16%)
    pallas_call x1, Pallas kernels, fused(): pl.pallas_call(kernel, out_shape=tuple((jax.ShapeDtypeStruct(x.shape, f32...  56.9 us
    unnamed x23, local copies, waits for them, and re-layouts  11 us

profile of v1, /device:TPU:0, one launch (start us, length us, event | category | flops | bytes accessed | tf_op | source)
XLA Modules:
  0.0 68.5 jit_solution(814012577776882012)
XLA Ops:
  0.6 0.0 copy-start
  0.6 0.9 %copy-done = f32[128,512]{1,0:T(8,128)S(1)} copy-done((f32[128,512]{1,0:T(8,128)S(1)}, f32[128,512]{1,0:T(8,128)}, u32[]{:S(2)}) %copy-start) | copy-done | bytes 262168
  1.6 0.0 copy-start.1
  1.6 0.9 %copy-done.1 = f32[4,128,128]{2,1,0:T(8,128)S(1)} copy-done((f32[4,128,128]{2,1,0:T(8,128)S(1)}, f32[4,128,128]{2,1,0:T(8,128)}, u32[]{:S(2)}) %copy-start.1) | copy-done | bytes 262168
  2.5 0.0 copy-start.2
  2.5 0.9 %copy-done.2 = f32[128,512]{1,0:T(8,128)S(1)} copy-done((f32[128,512]{1,0:T(8,128)S(1)}, f32[128,512]{1,0:T(8,128)}, u32[]{:S(2)}) %copy-start.2) | copy-done | bytes 262168
  3.5 0.0 copy-start.3
  3.5 0.9 %copy-done.3 = f32[4,128,128]{2,1,0:T(8,128)S(1)} copy-done((f32[4,128,128]{2,1,0:T(8,128)S(1)}, f32[4,128,128]{2,1,0:T(8,128)}, u32[]{:S(2)}) %copy-start.3) | copy-done | bytes 262168
  4.4 0.0 copy-start.4
  4.4 0.9 %copy-done.4 = f32[2,128,128]{2,1,0:T(8,128)S(1)} copy-done((f32[2,128,128]{2,1,0:T(8,128)S(1)}, f32[2,128,128]{2,1,0:T(8,128)}, u32[]{:S(2)}) %copy-start.4) | copy-done | bytes 131096
  5.3 0.0 copy-start.5
  5.3 0.9 %copy-done.5 = f32[128,256]{1,0:T(8,128)S(1)} copy-done((f32[128,256]{1,0:T(8,128)S(1)}, f32[128,256]{1,0:T(8,128)}, u32[]{:S(2)}) %copy-start.5) | copy-done | bytes 131096
  6.2 0.0 copy-start.6
  6.2 0.7 copy-done.6
  6.9 0.0 copy-start.7
  6.9 0.7 copy-done.7
  7.6 0.0 copy-start.8
  7.6 0.7 copy-done.8
  8.2 56.9 %shard_map.128 = (f32[128,256]{1,0:T(8,128)S(1)}, f32[2,128,128]{2,1,0:T(8,128)S(1)}, f32[128,512]{1,0:T(8,128)S(1)}, f32[4,128,128]{2,1,0:T(8,128)S(1)}, f32[4,128,128]{2,1,0:T(8,128)S(1)}) custom-call(f32[128,512]{1,0:T(8,128)S(1)} %copy-done, f32[2,128,128]{2,1,0:T(8,128)S(1)} %copy-done.4, f32[128,256]{1,0:T(8,128)S(1)} %copy-done.5, ...), custom_call_target="tpu_custom_call" | custom-call | tf_op jit(solution)/shard_map/pallas_call | solution.py:357
  65.1 0.7 copy.19
  65.7 0.7 copy.20
  66.4 0.7 %copy.21 = f32[128,512]{1,0:T(8,128)} copy(f32[128,512]{1,0:T(8,128)S(1)} %get-tuple-element.12) | data formatting | bytes 524288
  67.1 0.7 %copy.22 = f32[4,128,128]{2,1,0:T(8,128)} copy(f32[4,128,128]{2,1,0:T(8,128)S(1)} %get-tuple-element.13) | data formatting | bytes 524288
  67.8 0.7 %copy.23 = f32[4,128,128]{2,1,0:T(8,128)} copy(f32[4,128,128]{2,1,0:T(8,128)S(1)} %get-tuple-element.14) | data formatting | bytes 524288
Async XLA Ops:
  0.6 1.0 %copy-start = (f32[128,512]{1,0:T(8,128)S(1)}, f32[128,512]{1,0:T(8,128)}, u32[]{:S(2)}) copy-start(f32[128,512]{1,0:T(8,128)} %inverse.1) | copy-start | bytes 786436
  1.6 0.9 %copy-start.1 = (f32[4,128,128]{2,1,0:T(8,128)S(1)}, f32[4,128,128]{2,1,0:T(8,128)}, u32[]{:S(2)}) copy-start(f32[4,128,128]{2,1,0:T(8,128)} %pivots_zero.1) | copy-start | bytes 786436
  2.5 0.9 %copy-start.2 = (f32[128,512]{1,0:T(8,128)S(1)}, f32[128,512]{1,0:T(8,128)}, u32[]{:S(2)}) copy-start(f32[128,512]{1,0:T(8,128)} %factor_zero.1) | copy-start | bytes 786436
  3.5 0.9 %copy-start.3 = (f32[4,128,128]{2,1,0:T(8,128)S(1)}, f32[4,128,128]{2,1,0:T(8,128)}, u32[]{:S(2)}) copy-start(f32[4,128,128]{2,1,0:T(8,128)} %factor_parent.1) | copy-start | bytes 786436
  4.4 0.9 %copy-start.4 = (f32[2,128,128]{2,1,0:T(8,128)S(1)}, f32[2,128,128]{2,1,0:T(8,128)}, u32[]{:S(2)}) copy-start(f32[2,128,128]{2,1,0:T(8,128)} %pivots_one.1) | copy-start | bytes 393220
  5.3 0.9 %copy-start.5 = (f32[128,256]{1,0:T(8,128)S(1)}, f32[128,256]{1,0:T(8,128)}, u32[]{:S(2)}) copy-start(f32[128,256]{1,0:T(8,128)} %factor_one.1) | copy-start | bytes 393220
  6.2 0.7 copy-start.6
  6.9 0.7 copy-start.7
  7.6 0.7 copy-start.8

commit v2 on v1

--- a/solution.py
+++ b/solution.py
@@ -118,6 +118,7 @@
     return (cross_one, diag_one, cross_zero, parent_zero, diag_zero)
 
 
+VMEM_BYTES = 64 * 1024 * 1024
 RING = 8
 OWN = 3
 HALF = 5
@@ -140,12 +141,13 @@
 
 
 def kernel(
-    inverse, pivots_one, factor_one, pattern_one, pivots_zero, factor_zero, factor_parent, parent, pattern_zero,
-    cross_one, diag_one, cross_zero, parent_zero, diag_zero,
-    row, ones, ones_other, zeros, band, a_high, a_low, l_high, l_low, one_high, one_low, z, row_one, sums_one,
-    ring_send, ring_recv, pair_send, pair_recv,
+    inverse, pivots_one_hbm, factor_one_hbm, pattern_one, pivots_zero_hbm, factor_zero_hbm, factor_parent_hbm,
+    parent, pattern_zero, cross_one_hbm, diag_one_hbm, cross_zero_hbm, parent_zero_hbm, diag_zero_hbm,
+    cross_one, diag_one, cross_zero, parent_zero, diag_zero, pivots_one, factor_one, pivots_zero, factor_zero, factor_parent, row, ones, ones_other, zeros, band, a_high, a_low, l_high, l_low, one_high, one_low,
+    z, u, u_high, u_low, half_one, half_zero, mixed, row_one, sums_one,
+    ring_send, ring_recv, pair_send, pair_recv, load_done, store_done,
 ):
-    w = pivots_one.shape[1]
+    w = pivots_zero.shape[1]
     half_row = w // 2
     pole, prow, q = lax.axis_index("pole"), lax.axis_index("prow"), lax.axis_index("pcol")
     z_at, x_at = prow // 2, prow % 2
@@ -158,6 +160,22 @@
     for peer in (left, right, other):
         pl.semaphore_signal(barrier, inc=1, device_id=peer, device_id_type=pl.DeviceIdType.MESH)
 
+    loads = [
+        pltpu.make_async_copy(src, dst, load_done.at[n])
+        for n, (src, dst) in enumerate(
+            (
+                (factor_one_hbm, factor_one),
+                (factor_zero_hbm, factor_zero),
+                (inverse, row.at[q]),
+                (pivots_one_hbm, pivots_one.at[pl.ds(2 * q, 2)]),
+                (pivots_zero_hbm, pivots_zero),
+                (factor_parent_hbm, factor_parent),
+            )
+        )
+    ]
+    for load in loads:
+        load.start()
+
     def block(k):
         return slice(k * w, (k + 1) * w)
 
@@ -168,8 +186,10 @@
     parents = [parent[c] for c in range(4)]
     parent_mask = [sum(flag(p == k) * flag(pattern_one[0, k]) for k in range(4)) for p in parents]
     mask_zero = [flag(pattern_zero[0, c]) * parent_mask[c] for c in range(4)]
+    loads[0].wait()
     for k in range(2):
         ones[OWN, :, block(k)] = factor_one[:, block(k)] * mask_one[k]
+    loads[1].wait()
     for c in range(4):
         zeros[OWN, :, block(c)] = factor_zero[:, block(c)] * mask_zero[c]
 
@@ -196,12 +216,22 @@
             src, dst = band.at[slot, q], band.at[slot, q]
         elif slot == 0:
             src, dst = inverse, row.at[q]
-        elif slot == 1:
-            src, dst = row_one.at[pl.ds(2 * q, 2)], row_one.at[pl.ds(2 * q, 2)]
         else:
-            src, dst = sums_one.at[pl.ds(2 * q, 2)], sums_one.at[pl.ds(2 * q, 2)]
+            src, dst = pivots_one_hbm, pivots_one.at[pl.ds(2 * q, 2)]
         return copy(src, dst, pair_send.at[kind, slot], pair_recv.at[kind, slot], other)
 
+    stores = [
+        pltpu.make_async_copy(src, dst, store_done.at[n])
+        for n, (src, dst) in enumerate(
+            (
+                (cross_one, cross_one_hbm),
+                (diag_one, diag_one_hbm),
+                (cross_zero, cross_zero_hbm),
+                (parent_zero, parent_zero_hbm),
+                (diag_zero, diag_zero_hbm),
+            )
+        )
+    ]
     started = []
 
     def start(made):
@@ -214,8 +244,9 @@
         for way in (0, 1):
             start(to_ring(way, 1, chunk))
     start(to_pair(0, OWN))
-
-    row[q] = inverse[...]
+    start(to_pair(2, 1))
+
+    loads[2].wait()
     to_pair(2, 0).wait_recv()
     for d in range(HALF):
         column = natural((place + d) % RING)
@@ -234,39 +265,70 @@
             if 0 < d < HALF - 1:
                 a_high[block(u), block(t)], a_low[block(u), block(t)] = split(piece.T)
 
+    def take_half(t, blocks, column):
+        high, low = split(blocks[t])
+        lanes = pl.ds(pl.multiple_of(2 * column * w, 2 * w), 2 * w)
+        l_high[block(t), lanes], l_low[block(t), lanes] = high, low
+        for k in range(2):
+            one_high[2 * column + k, block(t), :] = high[:, block(k)]
+            one_low[2 * column + k, block(t), :] = low[:, block(k)]
+
     def take_ones(t):
-        high, low = split(ones[t])
-        l_high[block(t), : 2 * w], l_low[block(t), : 2 * w] = high, low
-        for k in range(2):
-            one_high[2 * q + k, block(t), :] = high[:, block(k)]
-            one_low[2 * q + k, block(t), :] = low[:, block(k)]
+        take_half(t, ones, q)
 
     def take_other(t):
-        high, low = split(ones_other[t])
-        for k in range(2):
-            one_high[2 * (1 - q) + k, block(t), :] = high[:, block(k)]
-            one_low[2 * (1 - q) + k, block(t), :] = low[:, block(k)]
+        take_half(t, ones_other, 1 - q)
 
     def take_zeros(t):
-        l_high[block(t), 2 * w :], l_low[block(t), 2 * w :] = split(zeros[t])
-
-    def times(rows, lo, hi):
+        l_high[block(t), 4 * w :], l_low[block(t), 4 * w :] = split(zeros[t])
+
+    def times(n, lo, hi):
         inner = slice(lo * w, hi * w)
-        return dot3((a_high[rows, inner], a_low[rows, inner]), (l_high[inner, :], l_low[inner, :]))
-
-    def add_old(lo, hi, new):
-        @pl.loop(lo, hi)
-        def _(t):
-            rows = pl.ds(pl.multiple_of(t * w, w), w)
-            total = z[rows, :]
-            for n in new:
-                total = total + times(rows, n, n + 1)
-            z[rows, :] = total
+        return dot3((a_high[block(n), inner], a_low[block(n), inner]), (l_high[inner, :], l_low[inner, :]))
+
+    across = ((0,), (0,))
+
+    def put(ref, k, value, first):
+        ref[k] = value if first else ref[k] + value
+
+    def absorb(n, lo, hi):
+        first = lo == hi
+        z[...] = times(n, n, n + 1)
+        if first:
+            for k in range(4):
+                row_one[k] = z[:, block(k)]
+            cross_zero[...] = z[:, 4 * w :]
+        else:
+            u[...] = times(n, lo, hi)
+            new = times(OWN, n, n + 1)
+            for k in range(4):
+                row_one[k] = row_one[k] + new[:, block(k)]
+                u_high[k], u_low[k] = split(u[:, block(k)])
+            cross_zero[...] = cross_zero[...] + new[:, 4 * w :]
+
+        def part(k, weight):
+            own = weight * z[:, block(k)]
+            return split(own if first else own + u[:, block(k)])
+
+        for k in range(8):
+            sums = dot3((l_high[block(n), block(k)], l_low[block(n), block(k)]), part(k, 0.5), across)
+            put(half_one if k < 4 else half_zero, k % 4, sums, first)
+        for c in range(4):
+            p = parents[c]
+            left_side = (one_high[p, block(n), :], one_low[p, block(n), :])
+            right_side = part(4 + c, 1.0)
+            if not first:
+                zeros_c = (l_high[block(n), block(4 + c)], l_low[block(n), block(4 + c)])
+                left_side = [jnp.concatenate(x, axis=0) for x in zip(left_side, (u_high[p], u_low[p]))]
+                right_side = [jnp.concatenate(x, axis=0) for x in zip(right_side, zeros_c)]
+            put(mixed, c, dot3(left_side, right_side, across), first)
 
     take_ones(OWN)
     take_zeros(OWN)
     take_band(OWN)
-    z[block(OWN), :] = times(block(OWN), OWN, OWN + 1)
+    to_pair(0, OWN).wait_recv()
+    take_other(OWN)
+    absorb(OWN, OWN, OWN)
 
     for step in range(1, 4):
         last = step == 3
@@ -281,9 +343,6 @@
                 if chunk == 2:
                     start(to_pair(1, t))
         new = (OWN - step, OWN + step)
-        if step == 1:
-            to_pair(0, OWN).wait_recv()
-            take_other(OWN)
         for t in new:
             take_ones(t)
             take_zeros(t)
@@ -291,9 +350,8 @@
             take_other(t)
             to_pair(1, t).wait_recv()
             take_band(t)
-        for t in new:
-            z[block(t), :] = times(block(t), OWN - step, OWN + step + 1)
-        add_old(OWN - step + 1, OWN + step, new)
+        absorb(OWN - step, OWN - step + 1, OWN + step)
+        absorb(OWN + step, OWN - step, OWN + step)
 
     far = RING - 1
     to_ring(1, 4, 0).wait_recv()
@@ -307,44 +365,47 @@
     take_other(far)
     to_pair(1, far).wait_recv()
     take_band(far)
-    add_old(0, far, (far,))
-    z[block(far), :] = times(block(far), 0, RING)
-
+    for load in loads[3:]:
+        load.wait()
+    to_pair(2, 1).wait_recv()
+    absorb(far, 0, far)
+
+    for k in range(4):
+        sums_one[k] = pivots_one[k] + half_one[k] + half_one[k].T
     for k in range(2):
-        row_one[2 * q + k] = z[block(OWN), block(k)]
-    start(to_pair(2, 1))
-    across = ((0,), (0,))
-    for k in range(2):
-        own = (l_high[:, block(k)], l_low[:, block(k)])
-        made = pivots_one[k] + dot3(own, split(z[:, block(k)]), across)
-        diag_one[k] = made
-        sums_one[2 * q + k] = made
-    start(to_pair(2, 2))
-    for k in range(2):
-        cross_one[:, block(k)] = -z[block(OWN), block(k)] * mask_one[k]
-
-    for c in range(4):
-        at = block(2 + c)
-        product = split(z[:, at])
-        p = parents[c]
-        zeros_c = (l_high[:, at], l_low[:, at])
-        parent_zero[c] = dot3((one_high[p], one_low[p]), product, across)
-        diag_zero[c] = pivots_zero[c] + dot3(zeros_c, product, across)
-
-    to_pair(2, 1).wait_recv()
-    to_pair(2, 2).wait_recv()
+        diag_one[k] = sums_one[2 * q + k]
+        cross_one[:, block(k)] = -row_one[2 * q + k] * mask_one[k]
+    stores[0].start()
+    stores[1].start()
     for c in range(4):
         p = parents[c]
         factor = split(factor_parent[c])
+        weight = mixed[c]
         lift = dot3(split(row_one[p]), factor)
-        cross_zero[:, block(c)] = (lift - z[block(OWN), block(2 + c)]) * mask_zero[c]
-        weight = parent_zero[c]
+        cross_zero[:, block(c)] = (lift - cross_zero[:, block(c)]) * mask_zero[c]
         sums = weight - dot3(split(sums_one[p]), factor)
         parent_zero[c] = sums
-        diag_zero[c] = diag_zero[c] - dot3(split(weight), factor, across) - dot3(factor, split(sums), across)
-
+        own = pivots_zero[c] + half_zero[c] + half_zero[c].T
+        diag_zero[c] = own - dot3(split(weight), factor, across) - dot3(factor, split(sums), across)
+    for store_out in stores[2:]:
+        store_out.start()
     for made in started:
         made.wait_send()
+    for store_out in stores:
+        store_out.wait()
+
+
+def store(*refs):
+    ins, outs, held, (load_done, store_done) = refs[:5], refs[5:10], refs[10:15], refs[15:]
+    loads = [pltpu.make_async_copy(ins[n], held[n], load_done.at[n]) for n in range(5)]
+    stores = [pltpu.make_async_copy(held[n], outs[n], store_done.at[n]) for n in range(5)]
+    for load in loads:
+        load.start()
+    for load, out in zip(loads, stores):
+        load.wait()
+        out.start()
+    for out in stores:
+        out.wait()
 
 
 def fused(*args):
@@ -353,13 +414,17 @@
     rows = RING * w
     f32, b16 = jnp.float32, jnp.bfloat16
     vmem, smem = pl.BlockSpec(memory_space=pltpu.VMEM), pl.BlockSpec(memory_space=pltpu.SMEM)
+    hbm = pl.BlockSpec(memory_space=pltpu.HBM)
     outs = (factor_one, pivots_one, factor_zero, factor_parent, pivots_zero)
-    return pl.pallas_call(
+    made = pl.pallas_call(
         kernel,
         out_shape=tuple(jax.ShapeDtypeStruct(x.shape, f32) for x in outs),
-        in_specs=[vmem, vmem, vmem, smem, vmem, vmem, vmem, smem, smem],
-        out_specs=(vmem,) * 5,
+        in_specs=[hbm, hbm, hbm, smem, hbm, hbm, hbm, smem, smem],
+        out_specs=(hbm,) * 5,
         scratch_shapes=[
+            *(pltpu.VMEM(x.shape, f32) for x in outs),
+            pltpu.VMEM((4, w, w), f32),
+            *(pltpu.VMEM(x.shape, f32) for x in (factor_one, pivots_zero, factor_zero, factor_parent)),
             pltpu.VMEM((2, w, 4 * w), f32),
             pltpu.VMEM((RING, w, 2 * w), f32),
             pltpu.VMEM((RING, w, 2 * w), f32),
@@ -367,22 +432,38 @@
             pltpu.VMEM((RING, 2, w // 2, HALF * w), f32),
             pltpu.VMEM((rows, rows), b16),
             pltpu.VMEM((rows, rows), b16),
-            pltpu.VMEM((rows, 6 * w), b16),
-            pltpu.VMEM((rows, 6 * w), b16),
+            pltpu.VMEM((rows, 8 * w), b16),
+            pltpu.VMEM((rows, 8 * w), b16),
             pltpu.VMEM((4, rows, w), b16),
             pltpu.VMEM((4, rows, w), b16),
-            pltpu.VMEM((rows, 6 * w), f32),
-            pltpu.VMEM((4, w, w), f32),
-            pltpu.VMEM((4, w, w), f32),
+            pltpu.VMEM((w, 8 * w), f32),
+            pltpu.VMEM((w, 8 * w), f32),
+            pltpu.VMEM((4, w, w), b16),
+            pltpu.VMEM((4, w, w), b16),
+            *(pltpu.VMEM((4, w, w), f32) for _ in range(5)),
             pltpu.SemaphoreType.DMA((2, 4, 3)),
             pltpu.SemaphoreType.DMA((2, 4, 3)),
             pltpu.SemaphoreType.DMA((3, RING)),
             pltpu.SemaphoreType.DMA((3, RING)),
+            pltpu.SemaphoreType.DMA((6,)),
+            pltpu.SemaphoreType.DMA((5,)),
         ],
         compiler_params=pltpu.CompilerParams(
-            collective_id=0, has_side_effects=True, vmem_limit_bytes=48 * 1024 * 1024
+            collective_id=0, has_side_effects=True, vmem_limit_bytes=VMEM_BYTES
         ),
     )(*args)
+    return pl.pallas_call(
+        store,
+        out_shape=tuple(jax.ShapeDtypeStruct(x.shape, f32) for x in outs),
+        in_specs=[hbm] * 5,
+        out_specs=(hbm,) * 5,
+        scratch_shapes=[
+            *(pltpu.VMEM(x.shape, f32) for x in outs),
+            pltpu.SemaphoreType.DMA((5,)),
+            pltpu.SemaphoreType.DMA((5,)),
+        ],
+        compiler_params=pltpu.CompilerParams(vmem_limit_bytes=VMEM_BYTES),
+    )(*made)
 
 
 def solution(mesh):

time: 68.8 us -> 56.4 us (0.82)
  local copies, waits for them, and re-layouts: 11 us -> 0 us
  Pallas kernels: 56.9 us -> 55.1 us
    unnamed x23 -> x0, local copies, waits for them, and re-layouts: 11 us -> none
    pallas_call x1, Pallas kernels: 56.9 us -> 53.1 us  [fused(): pl.pallas_call(kernel, out_shape=tuple((jax.ShapeDtypeStruct(x.shape, f32...]
    pallas_call x0 -> x1, Pallas kernels: none -> 2.05 us  [fused(): pl.pallas_call(store, out_shape=tuple((jax.ShapeDtypeStruct(x.shape, f32)...]
where the time goes in v2:
time: 56.4 us; the launch traced here: 55.8 us
  Pallas kernels  55.1 us (98%)
  between operations  0.64 us (1%)
    pallas_call x1, Pallas kernels, fused(): pl.pallas_call(kernel, out_shape=tuple((jax.ShapeDtypeStruct(x.shape, f32...  53.1 us
    pallas_call x1, Pallas kernels, fused(): pl.pallas_call(store, out_shape=tuple((jax.ShapeDtypeStruct(x.shape, f32)...  2.05 us

profile of v2, /device:TPU:0, one launch (start us, length us, event | category | flops | bytes accessed | tf_op | source)
XLA Modules:
  0.0 55.8 jit_solution(17177249030953947877)
XLA Ops:
  0.6 53.1 %shard_map.128 = (f32[128,256]{1,0:T(8,128)}, f32[2,128,128]{2,1,0:T(8,128)}, f32[128,512]{1,0:T(8,128)}, f32[4,128,128]{2,1,0:T(8,128)}, f32[4,128,128]{2,1,0:T(8,128)}) custom-call(f32[128,512]{1,0:T(8,128)} %inverse.1, f32[2,128,128]{2,1,0:T(8,128)} %pivots_one_hbm.1, f32[128,256]{1,0:T(8,128)} %factor_one_hbm.1, s32[1,4]{1,0:T(1,128)} %pattern_one.1, ...), custom_call_target="tpu_custom_call" | custom-call | tf_op jit(solution)/shard_map/pallas_call | solution.py:419
  53.7 2.0 %shard_map.129 = (f32[128,256]{1,0:T(8,128)}, f32[2,128,128]{2,1,0:T(8,128)}, f32[128,512]{1,0:T(8,128)}, f32[4,128,128]{2,1,0:T(8,128)}, f32[4,128,128]{2,1,0:T(8,128)}) custom-call(f32[128,256]{1,0:T(8,128)} %get-tuple-element.10.refs_0_, f32[2,128,128]{2,1,0:T(8,128)} %get-tuple-element.11.refs_1_, f32[128,512]{1,0:T(8,128)} %get-tuple-element.12.refs_2_, ...), custom_call_target="tpu_custom_call" | custom-call | tf_op jit(solution)/shard_map/pallas_call | solution.py:455

commit v3 on v2

--- a/solution.py
+++ b/solution.py
@@ -148,7 +148,7 @@
     ring_send, ring_recv, pair_send, pair_recv, load_done, store_done,
 ):
     w = pivots_zero.shape[1]
-    half_row = w // 2
+    half_row, eighth = w // 2, w // 16
     pole, prow, q = lax.axis_index("pole"), lax.axis_index("prow"), lax.axis_index("pcol")
     z_at, x_at = prow // 2, prow % 2
     place = z_at + x_at * (RING - 1 - 2 * z_at)
@@ -240,9 +240,8 @@
 
     pl.semaphore_wait(barrier, 3)
     start(to_pair(2, 0))
-    for chunk in (0, 1):
-        for way in (0, 1):
-            start(to_ring(way, 1, chunk))
+    for way in (0, 1):
+        start(to_ring(way, 1, 0))
     start(to_pair(0, OWN))
     start(to_pair(2, 1))
 
@@ -253,17 +252,36 @@
         source = (column // 4, slice(None), pl.ds(pl.multiple_of((column % 4) * w, w), w))
         piece = row[source]
         for h in range(2):
-            band[OWN, h, :, block(d)] = piece[h * half_row : (h + 1) * half_row]
-    for way in (0, 1):
-        start(to_ring(way, 1, 2))
+            if d < HALF - 1:
+                band[OWN, h, :half_row, block(d)] = piece[h * half_row : (h + 1) * half_row]
+            else:
+                sent = jnp.where(place < RING // 2, piece[:half_row], piece.T[half_row:])
+                for n in range(4):
+                    at = (4 * h + n) * eighth
+                    band[OWN, h, half_row:, block(n)] = sent[at : at + eighth]
+    for chunk in (2, 1):
+        for way in (0, 1):
+            start(to_ring(way, 1, chunk))
 
     def take_band(t):
-        for d in range(HALF):
-            piece = jnp.concatenate([band[t, h, :, block(d)] for h in range(2)], axis=0)
+        for d in range(HALF - 1):
+            piece = jnp.concatenate([band[t, h, :half_row, block(d)] for h in range(2)], axis=0)
             u = (t + d) % RING
             a_high[block(t), block(u)], a_low[block(t), block(u)] = split(piece)
-            if 0 < d < HALF - 1:
+            if d > 0:
                 a_high[block(u), block(t)], a_low[block(u), block(t)] = split(piece.T)
+
+    def take_pair(t):
+        u = t + RING // 2
+        low = (place + t + RING - OWN) % RING < RING // 2
+        at_t, at_u = (
+            jnp.concatenate([band[v, h, half_row:, block(n)] for h in range(2) for n in range(4)], axis=0)
+            for v in (t, u)
+        )
+        piece = jnp.concatenate([jnp.where(low, at_t, at_u), jnp.where(low, at_u, at_t)], axis=0)
+        turned = piece.T
+        a_high[block(t), block(u)], a_low[block(t), block(u)] = split(jnp.where(low, piece, turned))
+        a_high[block(u), block(t)], a_low[block(u), block(t)] = split(jnp.where(low, turned, piece))
 
     def take_half(t, blocks, column):
         high, low = split(blocks[t])
@@ -332,7 +350,7 @@
 
     for step in range(1, 4):
         last = step == 3
-        for chunk in (0, 1, 2):
+        for chunk in (0, 2, 1):
             for way in (0, 1):
                 to_ring(way, step, chunk).wait_recv()
                 t = OWN - step if way == 0 else OWN + step
@@ -350,6 +368,8 @@
             take_other(t)
             to_pair(1, t).wait_recv()
             take_band(t)
+        for t in ((), (1,), (0, 2))[step - 1]:
+            take_pair(t)
         absorb(OWN - step, OWN - step + 1, OWN + step)
         absorb(OWN + step, OWN - step, OWN + step)
 
@@ -365,6 +385,7 @@
     take_other(far)
     to_pair(1, far).wait_recv()
     take_band(far)
+    take_pair(OWN)
     for load in loads[3:]:
         load.wait()
     to_pair(2, 1).wait_recv()
@@ -377,18 +398,19 @@
         cross_one[:, block(k)] = -row_one[2 * q + k] * mask_one[k]
     stores[0].start()
     stores[1].start()
+    factors = [split(factor_parent[c]) for c in range(4)]
     for c in range(4):
         p = parents[c]
-        factor = split(factor_parent[c])
-        weight = mixed[c]
-        lift = dot3(split(row_one[p]), factor)
-        cross_zero[:, block(c)] = (lift - cross_zero[:, block(c)]) * mask_zero[c]
-        sums = weight - dot3(split(sums_one[p]), factor)
-        parent_zero[c] = sums
-        own = pivots_zero[c] + half_zero[c] + half_zero[c].T
-        diag_zero[c] = own - dot3(split(weight), factor, across) - dot3(factor, split(sums), across)
-    for store_out in stores[2:]:
-        store_out.start()
+        both = dot3(split(jnp.concatenate([row_one[p], sums_one[p]], axis=0)), factors[c])
+        cross_zero[:, block(c)] = (both[:w] - cross_zero[:, block(c)]) * mask_zero[c]
+        parent_zero[c] = mixed[c] - both[w:]
+    stores[2].start()
+    stores[3].start()
+    for c in range(4):
+        above = [jnp.concatenate(x, axis=0) for x in zip(split(mixed[c]), factors[c])]
+        below = [jnp.concatenate(x, axis=0) for x in zip(factors[c], split(parent_zero[c]))]
+        diag_zero[c] = pivots_zero[c] + half_zero[c] + half_zero[c].T - dot3(above, below, across)
+    stores[4].start()
     for made in started:
         made.wait_send()
     for store_out in stores:
@@ -429,7 +451,7 @@
             pltpu.VMEM((RING, w, 2 * w), f32),
             pltpu.VMEM((RING, w, 2 * w), f32),
             pltpu.VMEM((RING, w, 4 * w), f32),
-            pltpu.VMEM((RING, 2, w // 2, HALF * w), f32),
+            pltpu.VMEM((RING, 2, w // 2 + w // 16, 4 * w), f32),
             pltpu.VMEM((rows, rows), b16),
             pltpu.VMEM((rows, rows), b16),
             pltpu.VMEM((rows, 8 * w), b16),

time: 56.4 us -> 55.6 us (0.986)
  no operation moved by 1% of the time
where the time goes in v3:
time: 55.6 us; the launch traced here: 55.4 us
  Pallas kernels  54.7 us (98%)
  between operations  0.64 us (1%)
    pallas_call x1, Pallas kernels, fused(): pl.pallas_call(kernel, out_shape=tuple((jax.ShapeDtypeStruct(x.shape, f32...  52.7 us
    pallas_call x1, Pallas kernels, fused(): pl.pallas_call(store, out_shape=tuple((jax.ShapeDtypeStruct(x.shape, f32)...  2.05 us

profile of v3, /device:TPU:0, one launch (start us, length us, event | category | flops | bytes accessed | tf_op | source)
XLA Modules:
  0.0 55.4 jit_solution(15755529857394419645)
XLA Ops:
  0.6 52.7 %shard_map.128 = (f32[128,256]{1,0:T(8,128)}, f32[2,128,128]{2,1,0:T(8,128)}, f32[128,512]{1,0:T(8,128)}, f32[4,128,128]{2,1,0:T(8,128)}, f32[4,128,128]{2,1,0:T(8,128)}) custom-call(f32[128,512]{1,0:T(8,128)} %inverse.1, f32[2,128,128]{2,1,0:T(8,128)} %pivots_one_hbm.1, f32[128,256]{1,0:T(8,128)} %factor_one_hbm.1, s32[1,4]{1,0:T(1,128)} %pattern_one.1, ...), custom_call_target="tpu_custom_call" | custom-call | tf_op jit(solution)/shard_map/pallas_call | solution.py:441
  53.3 2.0 %shard_map.129 = (f32[128,256]{1,0:T(8,128)}, f32[2,128,128]{2,1,0:T(8,128)}, f32[128,512]{1,0:T(8,128)}, f32[4,128,128]{2,1,0:T(8,128)}, f32[4,128,128]{2,1,0:T(8,128)}) custom-call(f32[128,256]{1,0:T(8,128)} %get-tuple-element.10.refs_0_, f32[2,128,128]{2,1,0:T(8,128)} %get-tuple-element.11.refs_1_, f32[128,512]{1,0:T(8,128)} %get-tuple-element.12.refs_2_, ...), custom_call_target="tpu_custom_call" | custom-call | tf_op jit(solution)/shard_map/pallas_call | solution.py:477

commit v4 on v3

--- a/solution.py
+++ b/solution.py
@@ -350,16 +350,19 @@
 
     for step in range(1, 4):
         last = step == 3
-        for chunk in (0, 2, 1):
+        for chunk in (0, 2, 1) if step == 1 else (2, 0, 1):
             for way in (0, 1):
                 to_ring(way, step, chunk).wait_recv()
                 t = OWN - step if way == 0 else OWN + step
-                if not last or (chunk == 1) == (way == 0):
-                    start(to_ring(way, step + 1, chunk))
                 if chunk == 0:
                     start(to_pair(0, t))
                 if chunk == 2:
                     start(to_pair(1, t))
+                if not (step == 1 and chunk == 0) and (not last or (chunk == 1) == (way == 0)):
+                    start(to_ring(way, step + 1, chunk))
+            if step == 1 and chunk == 2:
+                for way in (0, 1):
+                    start(to_ring(way, 2, 0))
         new = (OWN - step, OWN + step)
         for t in new:
             take_ones(t)
@@ -374,18 +377,18 @@
         absorb(OWN + step, OWN - step, OWN + step)
 
     far = RING - 1
+    to_ring(1, 4, 2).wait_recv()
+    start(to_pair(1, far))
+    to_pair(1, far).wait_recv()
+    take_band(far)
+    take_pair(OWN)
     to_ring(1, 4, 0).wait_recv()
     start(to_pair(0, far))
     take_ones(far)
-    to_ring(1, 4, 2).wait_recv()
-    start(to_pair(1, far))
     to_ring(0, 4, 1).wait_recv()
     take_zeros(far)
     to_pair(0, far).wait_recv()
     take_other(far)
-    to_pair(1, far).wait_recv()
-    take_band(far)
-    take_pair(OWN)
     for load in loads[3:]:
         load.wait()
     to_pair(2, 1).wait_recv()

time: 55.6 us -> 55.4 us (level)
  no operation moved by 1% of the time
where the time goes in v4:
time: 55.4 us; the launch traced here: 55.2 us
  Pallas kernels  54.6 us (99%)
  between operations  0.64 us (1%)
    pallas_call x1, Pallas kernels, fused(): pl.pallas_call(kernel, out_shape=tuple((jax.ShapeDtypeStruct(x.shape, f32...  52.5 us
    pallas_call x1, Pallas kernels, fused(): pl.pallas_call(store, out_shape=tuple((jax.ShapeDtypeStruct(x.shape, f32)...  2.05 us

profile of v4, /device:TPU:0, one launch (start us, length us, event | category | flops | bytes accessed | tf_op | source)
XLA Modules:
  0.0 55.2 jit_solution(6317953277714855549)
XLA Ops:
  0.6 52.5 %shard_map.128 = (f32[128,256]{1,0:T(8,128)}, f32[2,128,128]{2,1,0:T(8,128)}, f32[128,512]{1,0:T(8,128)}, f32[4,128,128]{2,1,0:T(8,128)}, f32[4,128,128]{2,1,0:T(8,128)}) custom-call(f32[128,512]{1,0:T(8,128)} %inverse.1, f32[2,128,128]{2,1,0:T(8,128)} %pivots_one_hbm.1, f32[128,256]{1,0:T(8,128)} %factor_one_hbm.1, s32[1,4]{1,0:T(1,128)} %pattern_one.1, ...), custom_call_target="tpu_custom_call" | custom-call | tf_op jit(solution)/shard_map/pallas_call | solution.py:444
  53.2 2.0 %shard_map.129 = (f32[128,256]{1,0:T(8,128)}, f32[2,128,128]{2,1,0:T(8,128)}, f32[128,512]{1,0:T(8,128)}, f32[4,128,128]{2,1,0:T(8,128)}, f32[4,128,128]{2,1,0:T(8,128)}) custom-call(f32[128,256]{1,0:T(8,128)} %get-tuple-element.10.refs_0_, f32[2,128,128]{2,1,0:T(8,128)} %get-tuple-element.11.refs_1_, f32[128,512]{1,0:T(8,128)} %get-tuple-element.12.refs_2_, ...), custom_call_target="tpu_custom_call" | custom-call | tf_op jit(solution)/shard_map/pallas_call | solution.py:480
